TPU v7x, 32 devices: a whole 2x2x4 slice. The times are simulated.
32 devices in a mesh: loop: 8 (over z, core), chan: 4 (over y, x).
Axes of the slice: x: 2, y: 2, z: 4, core: 2. Of those that a mesh axis runs over, the one named last changes fastest.
Arguments:
- features: bfloat16 [32768, 256], P('loop', 'chan'), may hold values from -6 to 6
- kernel_tap_rows: float32 [9, 256], P(None, 'chan'), may hold values from -2 to 2
- in_weight: bfloat16 [256, 1024], replicated, may hold values from -0.375 to 0.375
- out_weight: bfloat16 [1024, 256], replicated, may hold values from -0.1875 to 0.1875
- cotangent: bfloat16 [32768, 256], P('loop', 'chan'), may hold values from -6 to 6
Outputs:
- block_out: bfloat16 [32768, 256], P('loop', 'chan')
- grad_features: bfloat16 [32768, 256], P('loop', 'chan')
- grad_in_weight: float32 [256, 1024], P('chan', 'loop')
- grad_out_weight: float32 [1024, 256], P('loop', 'chan')
- grad_kernel: float32 [9, 256], P(None, 'chan')
All inputs are finite; a program needn't handle non-finite values.
Results may differ from a plain program's by a relative error of at most 0.017.
Values may be sent and summed in bfloat16 or wider, within the bound.
A program may use at most 64 MiB of HBM per device.

v0:
```python
import math

import jax
import jax.numpy as jnp
from jax import lax
from jax.sharding import PartitionSpec as P

TAPS = 9
DILATION_STEP = 512


gelu_scale = math.sqrt(2.0 / math.pi)
cubic_coef = 0.044715
epsilon = 1e-05


def with_halo(cells, sides, width):
    for axis, dim in sides:
        count = lax.axis_size(axis)
        head = lax.slice_in_dim(cells, 0, width, axis=dim)
        tail = lax.slice_in_dim(cells, cells.shape[dim] - width, cells.shape[dim], axis=dim)
        cells = jnp.concatenate(
            [
                lax.ppermute(tail, axis, [(i, (i + 1) % count) for i in range(count)]),
                cells,
                lax.ppermute(head, axis, [((i + 1) % count, i) for i in range(count)]),
            ],
            axis=dim,
        )
    return cells


def gelu_pair(inputs):
    inner_arg = gelu_scale * (inputs + cubic_coef * inputs * inputs * inputs)
    tangent = jnp.tanh(inner_arg)
    act_value = 0.5 * inputs * (1.0 + tangent)
    act_slope = 0.5 * (1.0 + tangent) + 0.5 * inputs * (1.0 - tangent * tangent) * gelu_scale * (
        1.0 + 3.0 * cubic_coef * inputs * inputs
    )
    return (act_value, act_slope)


def widen_rows(field_rows, reach_positions):
    return with_halo(field_rows, (("loop", 0),), reach_positions)


def shards(features, kernel_tap_rows, in_weight, out_weight, cotangent):
    middle_position = (TAPS - 1) // 2
    reach_positions = middle_position * DILATION_STEP
    loop_size = lax.axis_size("loop")
    chan_size = lax.axis_size("chan")
    rows_here = features.shape[0]
    grad_scale = 1.0 / math.sqrt(rows_here * loop_size)
    padded_in = widen_rows(features, reach_positions)
    blended_sum = jnp.zeros(features.shape, jnp.float32)
    for kernel_tap_index in range(TAPS):
        leading_row = reach_positions + (kernel_tap_index - middle_position) * DILATION_STEP
        blended_sum = blended_sum + kernel_tap_rows[kernel_tap_index] * padded_in[
            leading_row : leading_row + rows_here
        ].astype(jnp.float32)
    filtered = blended_sum.astype(jnp.bfloat16)
    row_block, upstream = (
        lax.all_to_all(filtered, "chan", split_axis=0, concat_axis=1, tiled=True),
        lax.all_to_all(cotangent, "chan", split_axis=0, concat_axis=1, tiled=True),
    )
    values = row_block.astype(jnp.float32)
    mean_value = jnp.mean(values, axis=-1, keepdims=True)
    centred = values - mean_value
    variance = jnp.mean(centred * centred, axis=-1, keepdims=True)
    inv_std = lax.rsqrt(variance + epsilon)
    normed = centred * inv_std
    normed_b = normed.astype(jnp.bfloat16)
    hidden_pre = jnp.dot(normed_b, in_weight, preferred_element_type=jnp.float32)
    act_value, act_slope = gelu_pair(hidden_pre)
    act_b = act_value.astype(jnp.bfloat16)
    branch = jnp.dot(act_b, out_weight, preferred_element_type=jnp.float32).astype(jnp.bfloat16)
    grad_act = jnp.einsum("pc,fc->pf", upstream, out_weight, preferred_element_type=jnp.float32)
    grad_pre = (grad_act * act_slope).astype(jnp.bfloat16)
    grad_normed = jnp.einsum("pf,cf->pc", grad_pre, in_weight, preferred_element_type=jnp.float32)
    grad_filtered = inv_std * (
        grad_normed
        - jnp.mean(grad_normed, axis=-1, keepdims=True)
        - normed * jnp.mean(grad_normed * normed, axis=-1, keepdims=True)
    )
    back_rows = grad_filtered.astype(jnp.bfloat16)
    local_rows = row_block.shape[0]
    width_c = row_block.shape[1]
    width_f = hidden_pre.shape[1]
    chan_part = width_c // chan_size
    loop_part = width_f // loop_size
    normed_parts = normed_b.reshape(local_rows, chan_size, chan_part)
    upstream_parts = upstream.reshape(local_rows, chan_size, chan_part)
    grad_parts = grad_pre.reshape(local_rows, loop_size, loop_part)
    act_parts = act_b.reshape(local_rows, loop_size, loop_part)
    term_in = (
        jnp.einsum("pai,pbj->baij", normed_parts, grad_parts, preferred_element_type=jnp.float32)
        * grad_scale
    )
    term_out = (
        jnp.einsum("pbj,pai->baji", act_parts, upstream_parts, preferred_element_type=jnp.float32)
        * grad_scale
    )
    branch_cols, back_cols = (
        lax.all_to_all(branch, "chan", split_axis=1, concat_axis=0, tiled=True),
        lax.all_to_all(back_rows, "chan", split_axis=1, concat_axis=0, tiled=True),
    )
    block_out = (features.astype(jnp.float32) + branch_cols.astype(jnp.float32)).astype(
        jnp.bfloat16
    )
    first_in, first_out = (
        lax.psum_scatter(
            term_in.astype(jnp.bfloat16), "chan", scatter_dimension=1, tiled=True
        ).astype(jnp.float32),
        lax.psum_scatter(
            term_out.astype(jnp.bfloat16), "chan", scatter_dimension=1, tiled=True
        ).astype(jnp.float32),
    )
    summed_in, summed_out = (
        lax.psum_scatter(first_in, "loop", scatter_dimension=0, tiled=True),
        lax.psum_scatter(first_out, "loop", scatter_dimension=0, tiled=True),
    )
    grad_in_weight = summed_in.reshape(chan_part, loop_part)
    grad_out_weight = summed_out.reshape(loop_part, chan_part)
    padded_back = widen_rows(back_cols, reach_positions)
    grad_sum_rows = cotangent.astype(jnp.float32)
    back_wide = back_cols.astype(jnp.float32)
    kernel_rows = []
    for kernel_tap_index in range(TAPS):
        shift_positions = (kernel_tap_index - middle_position) * DILATION_STEP
        first_back = reach_positions - shift_positions
        grad_sum_rows = grad_sum_rows + kernel_tap_rows[kernel_tap_index] * padded_back[
            first_back : first_back + rows_here
        ].astype(jnp.float32)
        first_in_row = reach_positions + shift_positions
        kernel_rows.append(
            jnp.sum(
                back_wide * padded_in[first_in_row : first_in_row + rows_here].astype(jnp.float32),
                axis=0,
            )
        )
    kernel_terms = jnp.stack(kernel_rows) * grad_scale
    grad_kernel = lax.psum(kernel_terms, "loop")
    return (
        block_out,
        grad_sum_rows.astype(jnp.bfloat16),
        grad_in_weight,
        grad_out_weight,
        grad_kernel,
    )


def solution(mesh):
    placed = (P("loop", "chan"), P(None, "chan"), P(), P(), P("loop", "chan"))
    return jax.shard_map(
        shards,
        mesh=mesh,
        in_specs=placed,
        out_specs=(
            P("loop", "chan"),
            P("loop", "chan"),
            P("chan", "loop"),
            P("loop", "chan"),
            P(None, "chan"),
        ),
        check_vma=False,
    )
```

profile of v0, /device:TPU:0, one launch (start us, length us, event | category | flops | bytes accessed | tf_op | source)
XLA Modules:
  0.0 197.4 jit_solution(9589368475974990070)
XLA Ops:
  7.2 1.1 fusion.44
  8.3 0.5 collective-permute-start
  8.8 4.1 %collective-permute-start.1 = (bf16[2048,64]{0,1:T(8,128)(2,1)S(1)}, bf16[2048,64]{0,1:T(8,128)(2,1)S(1)}, u32[]{:S(2)}, u32[]{:S(2)}) collective-permute-start(bf16[2048,64]{0,1:T(8,128)(2,1)S(1)} %get-tuple-element.30), channel_id=1, source_target_pairs={{4,0},{8,4},{12,8},{16,12},{20,16},{24,20},{28,24},{0,28},{5,1},{9... | collective-permute-start | bytes 786440 | tf_op jit(solution)/shard_map/ppermute | solution.py:26
  12.9 1.0 slice_bitcast_fusion.10
  13.9 3.2 %collective-permute-done = bf16[2048,64]{0,1:T(8,128)(2,1)S(1)} collective-permute-done((bf16[2048,64]{0,1:T(8,128)(2,1)S(1)}, bf16[2048,64]{0,1:T(8,128)(2,1)S(1)}, u32[]{:S(2)}, u32[]{:S(2)}) %collective-permute-start) | collective-permute-done | bytes 262176 | tf_op jit(solution)/shard_map/ppermute | solution.py:24
  17.1 1.1 constant_dynamic-update-slice_fusion
  18.3 2.2 %fusion.19 = bf16[4096,64]{0,1:T(8,128)(2,1)S(1)} fusion(bf16[4096,64]{0,1:T(8,128)(2,1)} %param.5, f32[64]{0:T(128)S(1)} %get-tuple-element.38, f32[64]{0:T(128)S(1)} %get-tuple-element.39, f32[64]{0:T(128)S(1)} %get-tuple-element.32, f32[64]{0:T(128)S(1)} %get-tuple-element.33, f32[64]{0:T(128)S(1)} %get-tuple-element.34, f32[64]{0:T(128)S(1)} %get-tuple-element.35, ...), kind=kLoop, calls=%fused_computation.45 | loop fusion | flops 7077888 | bytes 5245184 | tf_op jit(solution)/shard_map/convert_element_type | solution.py:61
  20.5 0.8 copy.52
  21.3 4.7 %all-to-all-start = ((bf16[4,1024,64]{1,2,0:T(8,128)(2,1)}), bf16[4,1024,64]{1,2,0:T(8,128)(2,1)S(1)}, u32[]{:S(2)}, u32[]{:S(2)}) async-start(bf16[4,1024,64]{1,2,0:T(8,128)(2,1)} %bitcast.114), calls=%async_computation | async-start | bytes 1048576 | tf_op jit(solution)/shard_map/all_to_all | solution.py:63
  26.0 0.8 copy.51
  26.8 8.1 %all-to-all-done = bf16[4,1024,64]{1,2,0:T(8,128)(2,1)S(1)} async-done(((bf16[4,1024,64]{1,2,0:T(8,128)(2,1)}), bf16[4,1024,64]{1,2,0:T(8,128)(2,1)S(1)}, u32[]{:S(2)}, u32[]{:S(2)}) %all-to-all-start) | async-done | bytes 524320 | tf_op jit(solution)/shard_map/all_to_all | solution.py:63
  34.9 3.5 %all-to-all-start.2 = ((bf16[4,1024,64]{1,2,0:T(8,128)(2,1)}), bf16[4,1024,64]{1,2,0:T(8,128)(2,1)S(1)}, u32[]{:S(2)}, u32[]{:S(2)}) async-start(bf16[4,1024,64]{1,2,0:T(8,128)(2,1)} %bitcast.113), calls=%async_computation.2 | async-start | bytes 1048576 | tf_op jit(solution)/shard_map/all_to_all | solution.py:64
  38.4 0.1 convert_reduce_fusion
  38.5 0.2 multiply_reduce_fusion.1
  38.7 0.1 fusion.37
  38.8 4.2 %multiply_convert_fusion = (bf16[1024,1024]{0,1:T(8,128)(2,1)}, f32[1024,1024]{0,1:T(8,128)}) fusion(bf16[1024,256]{0,1:T(8,128)(2,1)S(1)} %fusion.37, bf16[256,1024]{1,0:T(8,128)(2,1)S(1)} %copy-done), kind=kOutput, calls=%fused_computation.9 | convolution fusion | flops 546308096 | bytes 7340032 | tf_op jit(solution)/shard_map/dot_general | solution.py:73
  43.0 3.5 %all-to-all-done.2 = bf16[4,1024,64]{1,2,0:T(8,128)(2,1)S(1)} async-done(((bf16[4,1024,64]{1,2,0:T(8,128)(2,1)}), bf16[4,1024,64]{1,2,0:T(8,128)(2,1)S(1)}, u32[]{:S(2)}, u32[]{:S(2)}) %all-to-all-start.2) | async-done | bytes 524320 | tf_op jit(solution)/shard_map/all_to_all | solution.py:64
  46.5 4.7 %fusion.6 = bf16[1024,1024]{0,1:T(8,128)(2,1)S(1)} fusion(f32[1024,1024]{0,1:T(8,128)} %get-tuple-element.42, bf16[1024,256]{1,0:T(8,128)(2,1)} %param.8, bf16[1024,256]{0,1:T(8,128)(2,1)S(1)} %bitcast.124), kind=kOutput, calls=%fused_computation.8 | convolution fusion | flops 556793856 | bytes 7340032 | tf_op jit(solution)/shard_map/pc,fc->pf/dot_general | solution.py:77
  51.2 0.8 fusion.43
  52.0 1.1 multiply_convert_fusion.2
  53.1 3.5 %all-to-all-start.3 = ((bf16[1024,4,64]{0,2,1:T(8,128)(2,1)}), bf16[1024,4,64]{0,2,1:T(8,128)(2,1)S(1)}, u32[]{:S(2)}, u32[]{:S(2)}) async-start(bf16[1024,4,64]{0,2,1:T(8,128)(2,1)} %bitcast.122), calls=%async_computation.3 | async-start | bytes 1048576 | tf_op jit(solution)/shard_map/all_to_all | solution.py:105
  56.6 0.6 dynamic-slice
  57.2 3.2 %convolution_convert_fusion = bf16[1024,256]{0,1:T(8,128)(2,1)} fusion(bf16[1024,1024]{0,1:T(8,128)(2,1)} %get-tuple-element.41, bf16[1024,256]{1,0:T(8,128)(2,1)} %param.8), kind=kOutput, calls=%fused_computation.32 | convolution fusion | flops 537133056 | bytes 3145728 | tf_op jit(solution)/shard_map/dot_general | solution.py:76
  60.4 3.4 %all-to-all-done.3 = bf16[1024,4,64]{0,2,1:T(8,128)(2,1)S(1)} async-done(((bf16[1024,4,64]{0,2,1:T(8,128)(2,1)}), bf16[1024,4,64]{0,2,1:T(8,128)(2,1)S(1)}, u32[]{:S(2)}, u32[]{:S(2)}) %all-to-all-start.3) | async-done | bytes 524320 | tf_op jit(solution)/shard_map/all_to_all | solution.py:105
  63.9 4.1 %all-to-all-start.1 = ((bf16[1024,4,64]{0,2,1:T(8,128)(2,1)}), bf16[1024,4,64]{0,2,1:T(8,128)(2,1)}, u32[]{:S(2)}, u32[]{:S(2)}) async-start(bf16[1024,4,64]{0,2,1:T(8,128)(2,1)} %bitcast.125), calls=%async_computation.1 | async-start | bytes 1048576 | tf_op jit(solution)/shard_map/all_to_all | solution.py:104
  68.0 0.0 all-reduce.5.cloned.1.call-start
  68.0 3.2 %fusion.9 = bf16[8,4,128,64]{2,3,1,0:T(8,128)(2,1)} fusion(bf16[1024,8,128,1]{0,2,3,1:T(8,128)(2,1)} %bitcast.138, bf16[4,1024,64]{1,2,0:T(8,128)(2,1)} %copy-done.5), kind=kOutput, calls=%fused_computation.35 | convolution fusion | flops 537395200 | bytes 3145728 | tf_op jit(solution)/shard_map/pbj,pai->baji/dot_general | solution.py:100
  71.3 3.2 %fusion.10 = bf16[8,4,64,128]{3,2,1,0:T(8,128)(2,1)} fusion(bf16[1024,8,128,1]{0,2,3,1:T(8,128)(2,1)} %bitcast.139, bf16[4,1024,64]{1,2,0:T(8,128)(2,1)S(1)} %all-to-all-done, f32[1024]{0:T(1024)S(1)} %add_rsqrt_fusion, f32[1024]{0:T(1024)S(1)} %broadcast_multiply_fusion.3), kind=kOutput, calls=%fused_computation.36 | convolution fusion | flops 538443776 | bytes 3153920 | tf_op jit(solution)/shard_map/pai,pbj->baij/dot_general | solution.py:96
  74.5 0.0 reduce-scatter.9.cloned.1.call-start
  74.5 1.1 copy.46
  75.6 1.1 convert_bitcast_fusion
  76.8 0.1 copy.45
  76.9 1.1 slice_bitcast_fusion.1
  78.0 0.1 collective-permute-start.3
  78.0 0.7 copy.47
  78.8 3.5 %collective-permute-start.2 = (bf16[2048,64]{0,1:T(8,128)(2,1)}, bf16[2048,64]{0,1:T(8,128)(2,1)}, u32[]{:S(2)}, u32[]{:S(2)}) collective-permute-start(bf16[2048,64]{0,1:T(8,128)(2,1)} %bitcast.71), channel_id=1, source_target_pairs={{4,0},{8,4},{12,8},{16,12},{20,16},{24,20},{28,24},{0,28},{5,1},{9... | collective-permute-start | bytes 786440 | tf_op jit(solution)/shard_map/ppermute | solution.py:26
  82.3 2.4 %fusion.35 = (f32[64]{0:T(128)S(1)}, f32[64]{0:T(128)S(1)}, f32[64]{0:T(128)S(1)}, f32[64]{0:T(128)S(1)}, f32[64]{0:T(128)S(1)}, /*index=5*/f32[64]{0:T(128)S(1)...) fusion(bf16[4096,64]{0,1:T(8,128)(2,1)S(1)} %bitcast.115, ...), kind=kLoop, calls=%fused_computation.61 | loop fusion | flops 7863744 | bytes 6818048 | tf_op jit(solution)/shard_map/reduce_sum | solution.py:136
  84.8 14.6 %psum.7 = f32[9,64]{1,0:T(8,128)} all-reduce(f32[9,64]{1,0:T(8,128)S(1)} %broadcast_multiply_fusion), channel_id=1, replica_groups=mesh['loop'=8,'chan'=4] {'loop'}, use_global_device_ids=true, to_apply=%region_17.0 | all-reduce | flops 576 | bytes 4608 | tf_op jit(solution)/shard_map/psum | solution.py:142
  99.4 1.0 constant_dynamic-update-slice_fusion.7
  100.4 25.8 %all-reduce.5.cloned.1.call-done = (bf16[8,4,64,128]{3,2,1,0:T(8,128)(2,1)}, bf16[8,4,128,64]{2,3,1,0:T(8,128)(2,1)}) async-done(((bf16[8,4,64,128]{3,2,1,0:T(8,128)(2,1)}, bf16[8,4,128,64]{2,3,1,0:T(8,128)(2,1)}), (bf16[8,4,64,128]{3,2,1,0:T(8,128)(2,1)}, bf16[8,4,128,64]{2,3,1,0:T(8,128)(2,1)})) %all-reduce.5.cloned.1.call-update) | async-done | bytes 1048592
  126.2 2.3 %dynamic-slice_convert_fusion.1 = f32[8,1,64,128]{3,2,1,0:T(8,128)} fusion(bf16[8,4,64,128]{3,2,1,0:T(8,128)(2,1)} %get-tuple-element.20, u32[]{:T(128)} %bitcast.56), kind=kLoop, calls=%fused_computation.80 | loop fusion | flops 65536 | bytes 393220 | tf_op jit(solution)/shard_map/convert_element_type | solution.py:113
  128.5 0.0 reduce-scatter.11.cloned.1.call-start
  128.6 0.1 constant_dynamic-update-slice_fusion.5
  128.7 1.0 constant_dynamic-update-slice_fusion.4
  129.6 2.3 %dynamic-slice_convert_fusion = f32[8,1,128,64]{2,3,1,0:T(8,128)} fusion(bf16[8,4,128,64]{2,3,1,0:T(8,128)(2,1)} %get-tuple-element.21, u32[]{:T(128)} %bitcast.56), kind=kLoop, calls=%fused_computation.79 | loop fusion | flops 65536 | bytes 393220 | tf_op jit(solution)/shard_map/convert_element_type | solution.py:116
  132.0 1.9 fusion.26
  133.9 25.5 %reduce-scatter.9.cloned.1.call-done = f32[1,1,64,128]{3,2,1,0:T(8,128)} async-done(((f32[8,1,64,128]{3,2,1,0:T(8,128)}), f32[1,1,64,128]{3,2,1,0:T(8,128)}) %reduce-scatter.9.cloned.1.call-update) | async-done | bytes 32784 | tf_op jit(solution)/shard_map/reduce_scatter | solution.py:119
  159.4 31.5 %reduce-scatter.11.cloned.1.call-done = f32[1,1,128,64]{2,3,1,0:T(8,128)} async-done(((f32[8,1,128,64]{2,3,1,0:T(8,128)}), f32[1,1,128,64]{2,3,1,0:T(8,128)}) %reduce-scatter.11.cloned.1.call-update) | async-done | bytes 32784 | tf_op jit(solution)/shard_map/reduce_scatter | solution.py:120
  (31 shorter events, 0.2 us)
Async XLA Ops:
  7.2 31.6 %copy-start = (bf16[256,1024]{1,0:T(8,128)(2,1)S(1)}, bf16[256,1024]{1,0:T(8,128)(2,1)}, u32[]{:S(2)}) copy-start(bf16[256,1024]{1,0:T(8,128)(2,1)} %param.7) | copy-start | bytes 1572868
  8.3 8.8 %collective-permute-start = (bf16[2048,64]{0,1:T(8,128)(2,1)S(1)}, bf16[2048,64]{0,1:T(8,128)(2,1)S(1)}, u32[]{:S(2)}, u32[]{:S(2)}) collective-permute-start(bf16[2048,64]{0,1:T(8,128)(2,1)S(1)} %get-tuple-element.29), channel_id=1, source_target_pairs={{0,4},{4,8},{8,12},{12,16},{16,20},{20,24},{24,28},{28,0},{1,5},{5... | collective-permute-start | bytes 786440 | tf_op jit(solution)/shard_map/ppermute | solution.py:24
  8.8 9.5 %collective-permute-start.1 = (bf16[2048,64]{0,1:T(8,128)(2,1)S(1)}, bf16[2048,64]{0,1:T(8,128)(2,1)S(1)}, u32[]{:S(2)}, u32[]{:S(2)}) collective-permute-start(bf16[2048,64]{0,1:T(8,128)(2,1)S(1)} %get-tuple-element.30), channel_id=1, source_target_pairs={{4,0},{8,4},{12,8},{16,12},{20,16},{24,20},{28,24},{0,28},{5,1},{9... | collective-permute-start | bytes 786440 | tf_op jit(solution)/shard_map/ppermute | solution.py:26
  18.3 7.7 %copy-start.3 = (bf16[4096,64]{0,1:T(8,128)(2,1)S(1)}, bf16[4096,64]{0,1:T(8,128)(2,1)}, u32[]{:S(2)}) copy-start(bf16[4096,64]{0,1:T(8,128)(2,1)} %param.9) | copy-start | bytes 1572868
  21.3 13.6 %all-to-all-start = ((bf16[4,1024,64]{1,2,0:T(8,128)(2,1)}), bf16[4,1024,64]{1,2,0:T(8,128)(2,1)S(1)}, u32[]{:S(2)}, u32[]{:S(2)}) async-start(bf16[4,1024,64]{1,2,0:T(8,128)(2,1)} %bitcast.114), calls=%async_computation | async-start | bytes 1048576 | tf_op jit(solution)/shard_map/all_to_all | solution.py:63
  34.9 11.6 %all-to-all-start.2 = ((bf16[4,1024,64]{1,2,0:T(8,128)(2,1)}), bf16[4,1024,64]{1,2,0:T(8,128)(2,1)S(1)}, u32[]{:S(2)}, u32[]{:S(2)}) async-start(bf16[4,1024,64]{1,2,0:T(8,128)(2,1)} %bitcast.113), calls=%async_computation.2 | async-start | bytes 1048576 | tf_op jit(solution)/shard_map/all_to_all | solution.py:64
  46.5 4.7 %copy-start.5 = (bf16[4,1024,64]{1,2,0:T(8,128)(2,1)}, bf16[4,1024,64]{1,2,0:T(8,128)(2,1)S(1)}, u32[]{:S(2)}) copy-start(bf16[4,1024,64]{1,2,0:T(8,128)(2,1)S(1)} %all-to-all-done.2) | copy-start | bytes 1572868
  51.2 1.9 copy-start.6
  51.2 5.4 %copy-start.7 = (u32[32]{0:T(128)S(1)}, u32[32]{0:T(128)}, u32[]{:S(2)}) copy-start(u32[32]{0:T(128)} %constant.26) | copy-start | bytes 388
  53.1 10.7 %all-to-all-start.3 = ((bf16[1024,4,64]{0,2,1:T(8,128)(2,1)}), bf16[1024,4,64]{0,2,1:T(8,128)(2,1)S(1)}, u32[]{:S(2)}, u32[]{:S(2)}) async-start(bf16[1024,4,64]{0,2,1:T(8,128)(2,1)} %bitcast.122), calls=%async_computation.3 | async-start | bytes 1048576 | tf_op jit(solution)/shard_map/all_to_all | solution.py:105
  63.8 7.4 %copy-start.2 = (bf16[1024,4,64]{0,2,1:T(8,128)(2,1)}, bf16[1024,4,64]{0,2,1:T(8,128)(2,1)S(1)}, u32[]{:S(2)}) copy-start(bf16[1024,4,64]{0,2,1:T(8,128)(2,1)S(1)} %all-to-all-done.3) | copy-start | bytes 1572868
  63.9 11.8 %all-to-all-start.1 = ((bf16[1024,4,64]{0,2,1:T(8,128)(2,1)}), bf16[1024,4,64]{0,2,1:T(8,128)(2,1)}, u32[]{:S(2)}, u32[]{:S(2)}) async-start(bf16[1024,4,64]{0,2,1:T(8,128)(2,1)} %bitcast.125), calls=%async_computation.1 | async-start | bytes 1048576 | tf_op jit(solution)/shard_map/all_to_all | solution.py:104
  68.0 58.2 %all-reduce.5.cloned.1.call-start = ((), (), s32[]{:S(2)}) async-start(), calls=%async_computation.8 | async-start | bytes 2097152
  74.4 7.9 %copy-start.1 = (bf16[4096,64]{0,1:T(8,128)(2,1)S(1)}, bf16[4096,64]{0,1:T(8,128)(2,1)}, u32[]{:S(2)}) copy-start(bf16[4096,64]{0,1:T(8,128)(2,1)} %param.5) | copy-start | bytes 1572868
  74.5 84.9 %reduce-scatter.9.cloned.1.call-start = ((), (), s32[]{:S(2)}) async-start(), calls=%async_computation.6 | async-start | bytes 294912 | tf_op jit(solution)/shard_map/reduce_scatter | solution.py:119
  78.0 21.4 %collective-permute-start.3 = (bf16[2048,64]{0,1:T(8,128)(2,1)S(1)}, bf16[2048,64]{0,1:T(8,128)(2,1)}, u32[]{:S(2)}, u32[]{:S(2)}) collective-permute-start(bf16[2048,64]{0,1:T(8,128)(2,1)S(1)} %bitcast.126), channel_id=1, source_target_pairs={{0,4},{4,8},{8,12},{12,16},{16,20},{20,24},{24,28},{28,0},{1,5},{5... | collective-permute-start | bytes 786440 | tf_op jit(solution)/shard_map/ppermute | solution.py:24
  78.8 49.9 %collective-permute-start.2 = (bf16[2048,64]{0,1:T(8,128)(2,1)}, bf16[2048,64]{0,1:T(8,128)(2,1)}, u32[]{:S(2)}, u32[]{:S(2)}) collective-permute-start(bf16[2048,64]{0,1:T(8,128)(2,1)} %bitcast.71), channel_id=1, source_target_pairs={{4,0},{8,4},{12,8},{16,12},{20,16},{24,20},{28,24},{0,28},{5,1},{9... | collective-permute-start | bytes 786440 | tf_op jit(solution)/shard_map/ppermute | solution.py:26
  84.7 47.2 %copy-start.4 = (bf16[4096,64]{0,1:T(8,128)(2,1)S(1)}, bf16[4096,64]{0,1:T(8,128)(2,1)}, u32[]{:S(2)}) copy-start(bf16[4096,64]{0,1:T(8,128)(2,1)} %param.9) | copy-start | bytes 1572868
  128.5 62.3 %reduce-scatter.11.cloned.1.call-start = ((), (), s32[]{:S(2)}) async-start(), calls=%async_computation.7 | async-start | bytes 294912 | tf_op jit(solution)/shard_map/reduce_scatter | solution.py:120
Sparse Core Ops, SparseCore 0:
  74.6 51.5 all-reduce.4
  129.0 30.3 reduce-scatter.8
  162.3 28.4 reduce-scatter.10
where the time goes:
time: 198 us; the launch traced here: 197 us
  waiting for transfers between devices  101 us (51%)
  starting transfers between devices  24.1 us (12%)
  matrix products  19.3 us (10%)
  blocking collectives  14.6 us (7%)
  between operations  14 us (7%)
  other arithmetic  13.7 us (7%)
  local copies, waits for them, and re-layouts  10.7 us (5%)
    reduce_scatter x1, waiting for transfers between devices, shards(): lax.psum_scatter(first_out, 'loop', scatter_dimension=0, tiled=True)  31.5 us
    unnamed x4, waiting for transfers between devices  25.9 us
    reduce_scatter x1, waiting for transfers between devices, shards(): lax.psum_scatter(first_in, 'loop', scatter_dimension=0, tiled=True)  25.5 us
    psum x1, blocking collectives, shards(): grad_kernel = lax.psum(kernel_terms, 'loop')  14.6 us
    all_to_all x1, waiting for transfers between devices, shards(): lax.all_to_all(filtered, 'chan', split_axis=0, concat_axis=1, tiled=True)  8.08 us
    ppermute x2, starting transfers between devices, with_halo(): lax.ppermute(head, axis, [((i + 1) % count, i) for i in range(count)])  7.63 us
    dot_general x1, matrix products, shards(): jnp.einsum('pc,fc->pf', upstream, out_weight, preferred_element_type=jnp....  4.71 us
    all_to_all x1, starting transfers between devices, shards(): lax.all_to_all(filtered, 'chan', split_axis=0, concat_axis=1, tiled=True)  4.68 us
  transfers between devices with their start and end apart: 11, of which 7 were waited for; matrix products, arithmetic and copies ran while one was open for 17% of the time, Pallas kernels for 0%

commit v1 on v0

--- a/solution.py
+++ b/solution.py
@@ -1,8 +1,11 @@
+import functools
 import math
 
 import jax
 import jax.numpy as jnp
 from jax import lax
+from jax.experimental import pallas as pl
+from jax.experimental.pallas import tpu as pltpu
 from jax.sharding import PartitionSpec as P
 
 TAPS = 9
@@ -149,10 +152,379 @@
     )
 
 
+MESH = pl.DeviceIdType.MESH
+MIDDLE = (TAPS - 1) // 2
+TILE_STEPS = 2
+SUB = 64
+
+
+def fused_kernel(
+    L, J, grad_scale,
+    x, ct, taps, win, wout,
+    bo_out, gx_out, gw_in_out, gw_out_out, gk_out,
+    tb, tf, xs, xr, xe, cs, cr, ctf, nb, nrm, istd, act, gp, ge,
+    bs, br, gs, gr, gfull, gsend, grecv, hf, hs, hr, sf, tr, kv, kp, kr, kt,
+    send, recv,
+):
+    rows, cl = x.shape
+    C = cl * J
+    F = win.shape[1]
+    R = DILATION_STEP // J
+    K = rows // DILATION_STEP
+    PAIRS = K // 2
+    TILE = 2 * R
+    Z = L // 2
+    own = MIDDLE * R
+    me_l, me_j = lax.axis_index("loop"), lax.axis_index("chan")
+    core, z = lax.rem(me_l, 2), me_l // 2
+    used = [0]
+
+    def take(n=1):
+        used[0] += n
+        return used[0] - n
+
+    def rcopy(src, dst, idx, l, j):
+        return pltpu.make_async_remote_copy(
+            src_ref=src, dst_ref=dst, send_sem=send.at[idx], recv_sem=recv.at[idx],
+            device_id=(l, j), device_id_type=MESH)
+
+    chan_peers = [lax.rem(me_j + d, J) for d in range(1, J)]
+    loop_peers = [lax.rem(me_l + e, L) for e in range(1, L)]
+    right, left = loop_peers[0], loop_peers[-1]
+
+    barrier = pltpu.get_barrier_semaphore()
+    for j in chan_peers:
+        pl.semaphore_signal(barrier, inc=1, device_id=(me_l, j), device_id_type=MESH)
+    for l in loop_peers:
+        pl.semaphore_signal(barrier, inc=1, device_id=(l, me_j), device_id_type=MESH)
+
+    def pack(src, dst):
+        for m in range(PAIRS):
+            for j in range(J):
+                a = 2 * m * DILATION_STEP + j * R
+                b = a + DILATION_STEP
+                dst[j, m * R:(m + 1) * R, :] = jnp.concatenate([src[a:a + R, :], src[b:b + R, :]], axis=1)
+
+    tb[me_j] = jnp.zeros((16, 128), jnp.float32)
+    tb[me_j, 0:TAPS, 0:cl] = taps[...]
+    pack(x, xs)
+    pl.semaphore_wait(barrier, J - 1 + L - 1)
+
+    pending = []
+
+    def to_chan(src, dst):
+        out = []
+        for j in chan_peers:
+            c = rcopy(src.at[j], dst.at[me_j], take(), me_l, j)
+            c.start()
+            out.append(c)
+        pending.extend(out)
+        return out
+
+    x_in = to_chan(xs, xr)
+    tap_in = []
+    for j in chan_peers:
+        c = rcopy(tb.at[me_j], tb.at[me_j], take(), me_l, j)
+        c.start()
+        tap_in.append(c)
+    pending.extend(tap_in)
+    pack(ct, cs)
+    ct_in = to_chan(cs, cr)
+
+    def unpack_full(buf, dst, base, m):
+        for h in range(2):
+            at = base + (2 * m + h) * R
+            dst[at:at + R, :] = jnp.concatenate(
+                [buf[s, m * R:(m + 1) * R, h * cl:(h + 1) * cl] for s in range(J)], axis=1)
+
+    xr[me_j] = xs[me_j]
+    for c in x_in:
+        c.wait_recv()
+    half = K // 2 * R
+    for m in range(PAIRS // 2):
+        unpack_full(xr, xe, own, m)
+    x_left = rcopy(xe.at[own:own + own], xe.at[own + K * R:2 * own + K * R], take(), left, me_j)
+    x_left.start()
+    for m in range(PAIRS // 2, PAIRS):
+        unpack_full(xr, xe, own, m)
+    x_right = rcopy(xe.at[K * R:own + K * R], xe.at[0:own], take(), right, me_j)
+    x_right.start()
+    for c in tap_in:
+        c.wait_recv()
+    tf[...] = jnp.concatenate([tb[s, :, 0:cl] for s in range(J)], axis=1)
+    cr[me_j] = cs[me_j]
+    for c in ct_in:
+        c.wait_recv()
+    for m in range(PAIRS):
+        unpack_full(cr, ctf, 0, m)
+    x_left.wait_recv()
+    x_right.wait_recv()
+    pending.extend([x_left, x_right])
+
+    bo_base = take(PAIRS * (J - 1))
+    ge_left = rcopy(ge.at[own:own + own], ge.at[own + K * R:2 * own + K * R], take(), left, me_j)
+    ge_right = rcopy(ge.at[K * R:own + K * R], ge.at[0:own], take(), right, me_j)
+    gs_base = take(PAIRS * (J - 1))
+    core_base = take(Z)
+
+    def tile_sends(src, dst, base, tile):
+        at = pl.ds(pl.multiple_of(tile * R, R), R)
+        return [rcopy(src.at[j, at], dst.at[me_j, at], base + tile * (J - 1) + d, me_l, j)
+                for d, j in enumerate(chan_peers)]
+
+    def tile_body(tile, carry):
+        base = pl.multiple_of(tile * TILE, TILE)
+        for b in range(TILE // SUB):
+            acc = jnp.zeros((SUB, C), jnp.float32)
+            for t in range(TAPS):
+                acc = acc + tf[t:t + 1, :] * xe[pl.ds(base + b * SUB + t * R, SUB), :].astype(jnp.float32)
+            v = acc.astype(jnp.bfloat16).astype(jnp.float32)
+            centred = v - jnp.mean(v, axis=-1, keepdims=True)
+            inv = lax.rsqrt(jnp.mean(centred * centred, axis=-1, keepdims=True) + epsilon)
+            normed = centred * inv
+            nrm[b * SUB:(b + 1) * SUB, :] = normed
+            istd[b * SUB:(b + 1) * SUB, :] = inv
+            nb[pl.ds(base + b * SUB, SUB), :] = normed.astype(jnp.bfloat16)
+        here = pl.ds(base, TILE)
+        normed_b = nb[here, :]
+        up = ctf[here, :]
+        FC = 256
+        for f in range(F // FC):
+            cols = slice(f * FC, (f + 1) * FC)
+            pre = jnp.dot(normed_b, win[:, cols], preferred_element_type=jnp.float32)
+            ga = lax.dot_general(up, wout[cols, :], (((1,), (1,)), ((), ())), preferred_element_type=jnp.float32)
+            sq = pre * pre
+            tangent = jnp.tanh(pre * (gelu_scale + (gelu_scale * cubic_coef) * sq))
+            gate = 0.5 + 0.5 * tangent
+            slope = gate + pre * (gate * (1.0 - tangent)) * (gelu_scale + (3.0 * gelu_scale * cubic_coef) * sq)
+            act[here, cols] = (pre * gate).astype(jnp.bfloat16)
+            gp[here, cols] = (ga * slope).astype(jnp.bfloat16)
+        gn = lax.dot_general(gp[here, :], win[...], (((1,), (1,)), ((), ())), preferred_element_type=jnp.float32)
+        for b in range(TILE // SUB):
+            s = slice(b * SUB, (b + 1) * SUB)
+            g, normed = gn[s], nrm[s, :]
+            out = istd[s, :] * (g - jnp.mean(g, axis=-1, keepdims=True)
+                                - normed * jnp.mean(g * normed, axis=-1, keepdims=True))
+            ge[pl.ds(own + base + b * SUB, SUB), :] = out.astype(jnp.bfloat16)
+
+        @pl.when(tile == PAIRS // 2 - 1)
+        def _():
+            ge_left.start()
+
+        @pl.when(tile == PAIRS - 1)
+        def _():
+            ge_right.start()
+
+        branch = jnp.dot(act[here, :], wout[...], preferred_element_type=jnp.float32).astype(jnp.bfloat16)
+        bo = (xe[pl.ds(own + base, TILE), :].astype(jnp.float32) + branch.astype(jnp.float32)).astype(jnp.bfloat16)
+        at = pl.ds(pl.multiple_of(tile * R, R), R)
+        for j in range(J):
+            bs[j, at, :] = jnp.concatenate([bo[0:R, j * cl:(j + 1) * cl], bo[R:, j * cl:(j + 1) * cl]], axis=1)
+        for c in tile_sends(bs, br, bo_base, tile):
+            c.start()
+        return carry
+
+    lax.fori_loop(0, PAIRS, tile_body, 0)
+
+    def term_body(zz, carry):
+        cols = pl.ds(pl.multiple_of(zz * 256, 256), 256)
+        for i, (a, b) in enumerate(((nb, gp), (ctf, act))):
+            term = lax.dot_general(a[...], b[:, cols], (((0,), (0,)), ((), ())),
+                                   preferred_element_type=jnp.float32) * grad_scale
+            for h in range(2):
+                part = term[:, h * 128:(h + 1) * 128]
+                gfull[h, zz, i] = part
+                gsend[h, zz, i] = part.astype(jnp.bfloat16)
+        rcopy(gsend.at[1 - core, zz], grecv.at[zz], core_base + zz, z * 2 + 1 - core, me_j).start()
+        return carry
+
+    lax.fori_loop(0, Z, term_body, 0)
+
+    def kernel_body(blk, carry):
+        base = pl.multiple_of(blk * SUB, SUB)
+        g = ge[pl.ds(own + base, SUB), :].astype(jnp.float32)
+        return tuple(
+            carry[t] + jnp.sum((g * xe[pl.ds(base + t * R, SUB), :].astype(jnp.float32)).reshape(SUB // 8, 8, C), axis=0)
+            for t in range(TAPS))
+
+    terms = lax.fori_loop(0, K * R // SUB, kernel_body,
+                          tuple(jnp.zeros((8, C), jnp.float32) for _ in range(TAPS)))
+    kv[...] = jnp.zeros_like(kv)
+    for t in range(TAPS):
+        kv[t:t + 1, :] = jnp.sum(terms[t], axis=0, keepdims=True) * grad_scale
+    for j in range(J):
+        kp[j] = jnp.concatenate([kv[:, j * cl:(j + 1) * cl], jnp.zeros((16, 128 - cl), jnp.float32)], axis=1)
+    k_in = to_chan(kp, kr)
+
+    ge_left.wait_recv()
+    ge_right.wait_recv()
+    pending.extend([ge_left, ge_right])
+
+    def back_body(tile, carry):
+        base = pl.multiple_of(tile * TILE, TILE)
+        for b in range(R // SUB):
+            pair = []
+            for h in range(2):
+                off = base + h * R + b * SUB
+                acc = ctf[pl.ds(off, SUB), :].astype(jnp.float32)
+                for t in range(TAPS):
+                    acc = acc + tf[t:t + 1, :] * ge[pl.ds(off + (TAPS - 1 - t) * R, SUB), :].astype(jnp.float32)
+                pair.append(acc.astype(jnp.bfloat16))
+            at = pl.ds(pl.multiple_of(tile * R, R) + b * SUB, SUB)
+            for j in range(J):
+                gs[j, at, :] = jnp.concatenate([p[:, j * cl:(j + 1) * cl] for p in pair], axis=1)
+        for c in tile_sends(gs, gr, gs_base, tile):
+            c.start()
+        return carry
+
+    lax.fori_loop(0, PAIRS, back_body, 0)
+
+    CR = C // J
+
+    def core_sum(zz, carry):
+        c = rcopy(gsend.at[1 - core, zz], grecv.at[zz], core_base + zz, z * 2 + 1 - core, me_j)
+        c.wait_recv()
+        c.wait_send()
+        for i in range(2):
+            h = gfull[core, zz, i] + grecv[zz, i].astype(jnp.float32)
+            for j in range(J):
+                hf[j, zz, i] = h[j * CR:(j + 1) * CR]
+                hs[j, zz, i] = h[j * CR:(j + 1) * CR].astype(jnp.bfloat16)
+        return carry
+
+    lax.fori_loop(0, Z, core_sum, 0)
+    h_in = to_chan(hs, hr)
+    for c in k_in:
+        c.wait_recv()
+    total = kp[me_j]
+    for d in range(1, J):
+        total = total + kr[lax.rem(me_j + J - d, J)]
+    kt[me_l] = total
+    kt_in = []
+    for l in loop_peers:
+        c = rcopy(kt.at[me_l], kt.at[me_l], take(), l, me_j)
+        c.start()
+        kt_in.append(c)
+    pending.extend(kt_in)
+
+    def finish(src, buf, base, out):
+        buf[me_j] = src[me_j]
+        for tile in range(PAIRS):
+            for c in tile_sends(src, buf, base, tile):
+                c.wait_recv()
+                c.wait_send()
+        for s in range(J):
+            for m in range(PAIRS):
+                for h in range(2):
+                    at = (2 * m + h) * DILATION_STEP + s * R
+                    out[at:at + R, :] = buf[s, m * R:(m + 1) * R, h * cl:(h + 1) * cl]
+
+    finish(bs, br, bo_base, bo_out)
+    for c in h_in:
+        c.wait_recv()
+    for zz in range(Z):
+        total = hf[me_j, zz]
+        for d in range(1, J):
+            total = total + hr[lax.rem(me_j + J - d, J), zz].astype(jnp.float32)
+        sf[zz] = total
+    z_in = []
+    for e in range(1, Z):
+        zz = lax.rem(z + e, Z)
+        c = rcopy(sf.at[zz], tr.at[z], take(), zz * 2 + core, me_j)
+        c.start()
+        z_in.append(c)
+    pending.extend(z_in)
+    finish(gs, gr, gs_base, gx_out)
+    for c in kt_in:
+        c.wait_recv()
+    total = kt[0]
+    for l in range(1, L):
+        total = total + kt[l]
+    gk_out[...] = total[0:TAPS, 0:cl]
+    for c in z_in:
+        c.wait_recv()
+    total = sf[z]
+    for e in range(1, Z):
+        total = total + tr[lax.rem(z + Z - e, Z)]
+    gw_in_out[...] = total[0]
+    gw_out_out[...] = total[1].T
+    for c in pending:
+        c.wait_send()
+
+
+def fits(L, J, rows, cl, F):
+    R = DILATION_STEP // J
+    return (cl * 2 == 128 and rows == 2 * MIDDLE * DILATION_STEP and L % 2 == 0 and L > 2 and J > 1
+            and F == L * 128 and R % SUB == 0)
+
+
+def fused_shards(features, kernel_tap_rows, in_weight, out_weight, cotangent):
+    L, J = lax.axis_size("loop"), lax.axis_size("chan")
+    rows, cl = features.shape
+    C, F = in_weight.shape
+    if not fits(L, J, rows, cl, F):
+        return shards(features, kernel_tap_rows, in_weight, out_weight, cotangent)
+    R = DILATION_STEP // J
+    K = rows // DILATION_STEP
+    N = K * R
+    Z = L // 2
+    CR = C // J
+    bf, f32 = jnp.bfloat16, jnp.float32
+    ext = N + 2 * MIDDLE * R
+    packed = pltpu.VMEM((J, N // 2, 128), bf)
+    scratch = [
+        pltpu.VMEM((J, 16, 128), f32),
+        pltpu.VMEM((16, C), f32),
+        packed, packed,
+        pltpu.VMEM((ext, C), bf),
+        packed, packed,
+        pltpu.VMEM((N, C), bf),
+        pltpu.VMEM((N, C), bf),
+        pltpu.VMEM((2 * R, C), f32),
+        pltpu.VMEM((2 * R, 1), f32),
+        pltpu.VMEM((N, F), bf),
+        pltpu.VMEM((N, F), bf),
+        pltpu.VMEM((ext, C), bf),
+        packed, packed,
+        packed, packed,
+        pltpu.VMEM((2, Z, 2, C, 128), f32),
+        pltpu.VMEM((2, Z, 2, C, 128), bf),
+        pltpu.VMEM((Z, 2, C, 128), bf),
+        pltpu.VMEM((J, Z, 2, CR, 128), f32),
+        pltpu.VMEM((J, Z, 2, CR, 128), bf),
+        pltpu.VMEM((J, Z, 2, CR, 128), bf),
+        pltpu.VMEM((Z, 2, CR, 128), f32),
+        pltpu.VMEM((Z, 2, CR, 128), f32),
+        pltpu.VMEM((16, C), f32),
+        pltpu.VMEM((J, 16, 128), f32),
+        pltpu.VMEM((J, 16, 128), f32),
+        pltpu.VMEM((L, 16, 128), f32),
+    ]
+    copies = (J - 1) * 5 + 4 + 2 * (K // 2) * (J - 1) + Z + (L - 1) + (Z - 1)
+    scratch += [pltpu.SemaphoreType.DMA((copies,)), pltpu.SemaphoreType.DMA((copies,))]
+    vmem = pl.BlockSpec(memory_space=pltpu.VMEM)
+    return pl.pallas_call(
+        functools.partial(fused_kernel, L, J, 1.0 / math.sqrt(rows * L)),
+        out_shape=(
+            jax.ShapeDtypeStruct((rows, cl), bf),
+            jax.ShapeDtypeStruct((rows, cl), bf),
+            jax.ShapeDtypeStruct((CR, F // L), f32),
+            jax.ShapeDtypeStruct((F // L, CR), f32),
+            jax.ShapeDtypeStruct((TAPS, cl), f32),
+        ),
+        in_specs=[vmem] * 5,
+        out_specs=(vmem,) * 5,
+        scratch_shapes=scratch,
+        compiler_params=pltpu.CompilerParams(
+            collective_id=0, has_side_effects=True, vmem_limit_bytes=50 * 1024 * 1024),
+        cost_estimate=pl.CostEstimate(flops=12 * N * C * F, bytes_accessed=8 * rows * cl * 2, transcendentals=N * F),
+    )(features, cotangent, kernel_tap_rows, in_weight, out_weight)
+
+
 def solution(mesh):
     placed = (P("loop", "chan"), P(None, "chan"), P(), P(), P("loop", "chan"))
     return jax.shard_map(
-        shards,
+        fused_shards,
         mesh=mesh,
         in_specs=placed,
         out_specs=(

time: 198 us -> 62.6 us (0.32)
  waiting for transfers between devices: 101 us -> 0 us
  Pallas kernels: 0 us -> 53.8 us
  starting transfers between devices: 24.1 us -> 0 us
  matrix products: 19.3 us -> 0 us
  blocking collectives: 14.6 us -> 0 us
  other arithmetic: 13.7 us -> 0 us
  between operations: 14 us -> 0.66 us
  local copies, waits for them, and re-layouts: 10.7 us -> 8 us
    reduce_scatter x2 -> x0, waiting for transfers between devices: 57 us -> none  [the longest x1 31.5 us: shards(): lax.psum_scatter(first_out, 'loop', scatter_dimension=0, tiled=True)]
    pallas_call x0 -> x1, Pallas kernels: none -> 53.8 us  [fused_shards(): pl.pallas_call(functools.partial(fused_kernel, L, J, 1.0 / math.sqrt(rows...]
    unnamed x4 -> x0, waiting for transfers between devices: 25.9 us -> none
    dot_general x6 -> x0, matrix products: 19.3 us -> none  [the longest x1 4.71 us: shards(): jnp.einsum('pc,fc->pf', upstream, out_weight, preferred_element_type=jnp....]
    all_to_all x4 -> x0, starting transfers between devices: 15.8 us -> none  [the longest x1 4.68 us: shards(): lax.all_to_all(filtered, 'chan', split_axis=0, concat_axis=1, tiled=True)]
    all_to_all x4 -> x0, waiting for transfers between devices: 15 us -> none  [the longest x1 8.08 us: shards(): lax.all_to_all(filtered, 'chan', split_axis=0, concat_axis=1, tiled=True)]
    psum x1 -> x0, blocking collectives: 14.6 us -> none  [shards(): grad_kernel = lax.psum(kernel_terms, 'loop')]
    convert_element_type x6 -> x0, other arithmetic: 9.81 us -> none  [the longest x2 4.57 us: shards(): first_in, first_out = (lax.psum_scatter(term_in.astype(jnp.bfloat16), 'ch...]
  transfers between devices with their start and end apart: 11 -> 0, of which waited for: 7 -> 0; matrix products, arithmetic and copies ran while one was open for 17% -> 0% of each run, Pallas kernels for 0% -> 0%
where the time goes in v1:
time: 62.6 us; the launch traced here: 62.4 us
  Pallas kernels  53.8 us (86%)
  local copies, waits for them, and re-layouts  8 us (13%)
  between operations  0.66 us (1%)
    pallas_call x1, Pallas kernels, fused_shards(): pl.pallas_call(functools.partial(fused_kernel, L, J, 1.0 / math.sqrt(rows...  53.8 us
    unnamed x12, local copies, waits for them, and re-layouts  4.99 us
    pallas_call x3, local copies, waits for them, and re-layouts, fused_shards(): pl.pallas_call(functools.partial(fused_kernel, L, J, 1.0 / math.sqrt(rows...  3.01 us

profile of v1, /device:TPU:0, one launch (start us, length us, event | category | flops | bytes accessed | tf_op | source)
XLA Modules:
  0.0 62.4 jit_solution(1722095284120950534)
XLA Ops:
  0.6 0.0 copy-start.3
  0.6 2.4 %copy.10.x = bf16[4096,64]{1,0:T(8,128)(2,1)} copy(bf16[4096,64]{0,1:T(8,128)(2,1)} %param.5) | data formatting | bytes 1048576 | tf_op args[0]
  3.0 0.0 copy-done.3
  3.1 0.0 copy-start
  3.1 0.0 copy-start.1
  3.1 0.0 copy-start.2
  3.1 1.4 %copy.11.ct = bf16[4096,64]{1,0:T(8,128)(2,1)} copy(bf16[4096,64]{0,1:T(8,128)(2,1)S(1)} %copy-done.3) | data formatting | bytes 1048576 | tf_op args[4]
  4.4 0.0 copy-done
  4.4 0.0 copy-done.1
  4.4 0.0 copy-done.2
  4.4 53.8 %shard_map.92 = (bf16[4096,64]{1,0:T(8,128)(2,1)S(1)}, bf16[4096,64]{1,0:T(8,128)(2,1)S(1)}, f32[64,128]{1,0:T(8,128)S(1)}, f32[128,64]{1,0:T(8,128)S(1)}, f32[9,64]{1,0:T(8,128)S(1)}) custom-call(bf16[4096,64]{1,0:T(8,128)(2,1)} %copy.10.x, bf16[4096,64]{1,0:T(8,128)(2,1)} %copy.11.ct, f32[9,64]{1,0:T(8,128)S(1)} %copy-done.2, ...), custom_call_target="tpu_custom_call" | custom-call | flops 3221225472 | bytes 4194304 | tf_op jit(solution)/shard_map/pallas_call | solution.py:506
  58.2 1.2 %copy.12 = bf16[4096,64]{0,1:T(8,128)(2,1)} copy(bf16[4096,64]{1,0:T(8,128)(2,1)S(1)} %get-tuple-element.5) | data formatting | bytes 1048576 | tf_op jit(solution)/shard_map/pallas_call | solution.py:506
  59.4 0.7 %copy.14 = f32[128,64]{0,1:T(8,128)} copy(f32[128,64]{1,0:T(8,128)S(1)} %get-tuple-element.8) | data formatting | bytes 65536 | tf_op jit(solution)/shard_map/pallas_call | solution.py:506
  60.1 1.2 %copy.13 = bf16[4096,64]{0,1:T(8,128)(2,1)} copy(bf16[4096,64]{1,0:T(8,128)(2,1)S(1)} %get-tuple-element.6) | data formatting | bytes 1048576 | tf_op jit(solution)/shard_map/pallas_call | solution.py:506
  61.2 0.6 copy.17
  61.8 0.6 copy.18
Async XLA Ops:
  0.6 2.4 %copy-start.3 = (bf16[4096,64]{0,1:T(8,128)(2,1)S(1)}, bf16[4096,64]{0,1:T(8,128)(2,1)}, u32[]{:S(2)}) copy-start(bf16[4096,64]{0,1:T(8,128)(2,1)} %param.9) | copy-start | bytes 1572868
  3.1 1.4 %copy-start = (bf16[256,1024]{1,0:T(8,128)(2,1)S(1)}, bf16[256,1024]{1,0:T(8,128)(2,1)}, u32[]{:S(2)}) copy-start(bf16[256,1024]{1,0:T(8,128)(2,1)} %win.1) | copy-start | bytes 1572868
  3.1 1.4 %copy-start.1 = (bf16[1024,256]{1,0:T(8,128)(2,1)S(1)}, bf16[1024,256]{1,0:T(8,128)(2,1)}, u32[]{:S(2)}) copy-start(bf16[1024,256]{1,0:T(8,128)(2,1)} %wout.1) | copy-start | bytes 1572868
  3.1 1.4 %copy-start.2 = (f32[9,64]{1,0:T(8,128)S(1)}, f32[9,64]{1,0:T(8,128)}, u32[]{:S(2)}) copy-start(f32[9,64]{1,0:T(8,128)} %taps.1) | copy-start | bytes 6916

commit v2 on v1

--- a/solution.py
+++ b/solution.py
@@ -155,18 +155,17 @@
 MESH = pl.DeviceIdType.MESH
 MIDDLE = (TAPS - 1) // 2
 TILE_STEPS = 2
-SUB = 64
 
 
 def fused_kernel(
     L, J, grad_scale,
     x, ct, taps, win, wout,
     bo_out, gx_out, gw_in_out, gw_out_out, gk_out,
-    tb, tf, xs, xr, xe, cs, cr, ctf, nb, nrm, istd, act, gp, ge,
-    bs, br, gs, gr, gfull, gsend, grecv, hf, hs, hr, sf, tr, kv, kp, kr, kt,
+    tb, tf, wint, woutt, xs, xe, cs, ctf, xr, nb, nrm, istd, act, gp, ge,
+    bs, br, gs, gr, gfull, gsend, grecv, hf, hs, hr, sf, tr, kp, kr, kt,
     send, recv,
 ):
-    rows, cl = x.shape
+    cl, rows = x.shape
     C = cl * J
     F = win.shape[1]
     R = DILATION_STEP // J
@@ -199,11 +198,10 @@
         pl.semaphore_signal(barrier, inc=1, device_id=(l, me_j), device_id_type=MESH)
 
     def pack(src, dst):
-        for m in range(PAIRS):
+        for k in range(K):
             for j in range(J):
-                a = 2 * m * DILATION_STEP + j * R
-                b = a + DILATION_STEP
-                dst[j, m * R:(m + 1) * R, :] = jnp.concatenate([src[a:a + R, :], src[b:b + R, :]], axis=1)
+                a = k * DILATION_STEP + j * R
+                dst[j, :, k * R:(k + 1) * R] = src[:, a:a + R]
 
     tb[me_j] = jnp.zeros((16, 128), jnp.float32)
     tb[me_j, 0:TAPS, 0:cl] = taps[...]
@@ -229,83 +227,81 @@
         tap_in.append(c)
     pending.extend(tap_in)
     pack(ct, cs)
-    ct_in = to_chan(cs, cr)
-
-    def unpack_full(buf, dst, base, m):
-        for h in range(2):
-            at = base + (2 * m + h) * R
-            dst[at:at + R, :] = jnp.concatenate(
-                [buf[s, m * R:(m + 1) * R, h * cl:(h + 1) * cl] for s in range(J)], axis=1)
-
+    ct_in = to_chan(cs, ctf)
+
+    wint[...] = win[...].T
+    woutt[...] = wout[...].T
     xr[me_j] = xs[me_j]
     for c in x_in:
         c.wait_recv()
-    half = K // 2 * R
-    for m in range(PAIRS // 2):
-        unpack_full(xr, xe, own, m)
-    x_left = rcopy(xe.at[own:own + own], xe.at[own + K * R:2 * own + K * R], take(), left, me_j)
+    for s in range(J):
+        xe[s * cl:(s + 1) * cl, own:own + K * R] = xr[s]
+    x_left = rcopy(xe.at[:, own:own + own], xe.at[:, own + K * R:2 * own + K * R], take(), left, me_j)
     x_left.start()
-    for m in range(PAIRS // 2, PAIRS):
-        unpack_full(xr, xe, own, m)
-    x_right = rcopy(xe.at[K * R:own + K * R], xe.at[0:own], take(), right, me_j)
+    x_right = rcopy(xe.at[:, K * R:own + K * R], xe.at[:, 0:own], take(), right, me_j)
     x_right.start()
     for c in tap_in:
         c.wait_recv()
-    tf[...] = jnp.concatenate([tb[s, :, 0:cl] for s in range(J)], axis=1)
-    cr[me_j] = cs[me_j]
+    columns = jnp.concatenate(
+        [jnp.concatenate([tb[s, :, 0:cl] for s in range(J)], axis=1), jnp.zeros((112, C), jnp.float32)], axis=0).T
+    for t in range(TAPS):
+        tf[t] = jnp.broadcast_to(columns[:, t:t + 1], (C, R))
+    ctf[me_j] = cs[me_j]
     for c in ct_in:
         c.wait_recv()
-    for m in range(PAIRS):
-        unpack_full(cr, ctf, 0, m)
     x_left.wait_recv()
     x_right.wait_recv()
     pending.extend([x_left, x_right])
 
     bo_base = take(PAIRS * (J - 1))
-    ge_left = rcopy(ge.at[own:own + own], ge.at[own + K * R:2 * own + K * R], take(), left, me_j)
-    ge_right = rcopy(ge.at[K * R:own + K * R], ge.at[0:own], take(), right, me_j)
+    ge_left = rcopy(ge.at[:, own:own + own], ge.at[:, own + K * R:2 * own + K * R], take(), left, me_j)
+    ge_right = rcopy(ge.at[:, K * R:own + K * R], ge.at[:, 0:own], take(), right, me_j)
     gs_base = take(PAIRS * (J - 1))
     core_base = take(Z)
 
     def tile_sends(src, dst, base, tile):
-        at = pl.ds(pl.multiple_of(tile * R, R), R)
-        return [rcopy(src.at[j, at], dst.at[me_j, at], base + tile * (J - 1) + d, me_l, j)
+        at = pl.ds(pl.multiple_of(tile * TILE, TILE), TILE)
+        return [rcopy(src.at[j, :, at], dst.at[me_j, :, at], base + tile * (J - 1) + d, me_l, j)
                 for d, j in enumerate(chan_peers)]
 
     def tile_body(tile, carry):
         base = pl.multiple_of(tile * TILE, TILE)
-        for b in range(TILE // SUB):
-            acc = jnp.zeros((SUB, C), jnp.float32)
-            for t in range(TAPS):
-                acc = acc + tf[t:t + 1, :] * xe[pl.ds(base + b * SUB + t * R, SUB), :].astype(jnp.float32)
-            v = acc.astype(jnp.bfloat16).astype(jnp.float32)
-            centred = v - jnp.mean(v, axis=-1, keepdims=True)
-            inv = lax.rsqrt(jnp.mean(centred * centred, axis=-1, keepdims=True) + epsilon)
+        for b in range(TILE_STEPS):
+            for j in range(J):
+                ch = slice(j * cl, (j + 1) * cl)
+                acc = jnp.zeros((cl, R), jnp.float32)
+                for t in range(TAPS):
+                    acc = acc + tf[t, ch, :] * xe[ch, pl.ds(base + (b + t) * R, R)].astype(jnp.float32)
+                nrm[ch, b * R:(b + 1) * R] = acc.astype(jnp.bfloat16).astype(jnp.float32)
+            here_b = slice(b * R, (b + 1) * R)
+            v = nrm[:, here_b]
+            centred = v - jnp.mean(v, axis=0, keepdims=True)
+            inv = lax.rsqrt(jnp.mean(centred * centred, axis=0, keepdims=True) + epsilon)
             normed = centred * inv
-            nrm[b * SUB:(b + 1) * SUB, :] = normed
-            istd[b * SUB:(b + 1) * SUB, :] = inv
-            nb[pl.ds(base + b * SUB, SUB), :] = normed.astype(jnp.bfloat16)
+            nrm[:, here_b] = normed
+            istd[:, here_b] = inv
+            nb[:, pl.ds(base + b * R, R)] = normed.astype(jnp.bfloat16)
         here = pl.ds(base, TILE)
-        normed_b = nb[here, :]
-        up = ctf[here, :]
+        normed_b = nb[:, here]
+        up = jnp.concatenate([ctf[j, :, here] for j in range(J)], axis=0)
         FC = 256
         for f in range(F // FC):
-            cols = slice(f * FC, (f + 1) * FC)
-            pre = jnp.dot(normed_b, win[:, cols], preferred_element_type=jnp.float32)
-            ga = lax.dot_general(up, wout[cols, :], (((1,), (1,)), ((), ())), preferred_element_type=jnp.float32)
+            part = slice(f * FC, (f + 1) * FC)
+            pre = jnp.dot(wint[part, :], normed_b, preferred_element_type=jnp.float32)
+            ga = jnp.dot(wout[part, :], up, preferred_element_type=jnp.float32)
             sq = pre * pre
             tangent = jnp.tanh(pre * (gelu_scale + (gelu_scale * cubic_coef) * sq))
             gate = 0.5 + 0.5 * tangent
             slope = gate + pre * (gate * (1.0 - tangent)) * (gelu_scale + (3.0 * gelu_scale * cubic_coef) * sq)
-            act[here, cols] = (pre * gate).astype(jnp.bfloat16)
-            gp[here, cols] = (ga * slope).astype(jnp.bfloat16)
-        gn = lax.dot_general(gp[here, :], win[...], (((1,), (1,)), ((), ())), preferred_element_type=jnp.float32)
-        for b in range(TILE // SUB):
-            s = slice(b * SUB, (b + 1) * SUB)
-            g, normed = gn[s], nrm[s, :]
-            out = istd[s, :] * (g - jnp.mean(g, axis=-1, keepdims=True)
-                                - normed * jnp.mean(g * normed, axis=-1, keepdims=True))
-            ge[pl.ds(own + base + b * SUB, SUB), :] = out.astype(jnp.bfloat16)
+            act[part, here] = (pre * gate).astype(jnp.bfloat16)
+            gp[part, here] = (ga * slope).astype(jnp.bfloat16)
+        gn = jnp.dot(win[...], gp[:, here], preferred_element_type=jnp.float32)
+        for b in range(TILE_STEPS):
+            s = slice(b * R, (b + 1) * R)
+            g, normed = gn[:, s], nrm[:, s]
+            out = istd[:, s] * (g - jnp.mean(g, axis=0, keepdims=True)
+                                - normed * jnp.mean(g * normed, axis=0, keepdims=True))
+            ge[:, pl.ds(own + base + b * R, R)] = out.astype(jnp.bfloat16)
 
         @pl.when(tile == PAIRS // 2 - 1)
         def _():
@@ -315,11 +311,10 @@
         def _():
             ge_right.start()
 
-        branch = jnp.dot(act[here, :], wout[...], preferred_element_type=jnp.float32).astype(jnp.bfloat16)
-        bo = (xe[pl.ds(own + base, TILE), :].astype(jnp.float32) + branch.astype(jnp.float32)).astype(jnp.bfloat16)
-        at = pl.ds(pl.multiple_of(tile * R, R), R)
+        branch = jnp.dot(woutt[...], act[:, here], preferred_element_type=jnp.float32).astype(jnp.bfloat16)
+        bo = (xe[:, pl.ds(own + base, TILE)].astype(jnp.float32) + branch.astype(jnp.float32)).astype(jnp.bfloat16)
         for j in range(J):
-            bs[j, at, :] = jnp.concatenate([bo[0:R, j * cl:(j + 1) * cl], bo[R:, j * cl:(j + 1) * cl]], axis=1)
+            bs[j, :, here] = bo[j * cl:(j + 1) * cl]
         for c in tile_sends(bs, br, bo_base, tile):
             c.start()
         return carry
@@ -328,8 +323,9 @@
 
     def term_body(zz, carry):
         cols = pl.ds(pl.multiple_of(zz * 256, 256), 256)
-        for i, (a, b) in enumerate(((nb, gp), (ctf, act))):
-            term = lax.dot_general(a[...], b[:, cols], (((0,), (0,)), ((), ())),
+        both = jnp.concatenate([ctf[j] for j in range(J)], axis=0)
+        for i, (a, b) in enumerate(((nb[...], gp), (both, act))):
+            term = lax.dot_general(a, b[cols, :], (((1,), (1,)), ((), ())),
                                    preferred_element_type=jnp.float32) * grad_scale
             for h in range(2):
                 part = term[:, h * 128:(h + 1) * 128]
@@ -340,20 +336,16 @@
 
     lax.fori_loop(0, Z, term_body, 0)
 
-    def kernel_body(blk, carry):
-        base = pl.multiple_of(blk * SUB, SUB)
-        g = ge[pl.ds(own + base, SUB), :].astype(jnp.float32)
-        return tuple(
-            carry[t] + jnp.sum((g * xe[pl.ds(base + t * R, SUB), :].astype(jnp.float32)).reshape(SUB // 8, 8, C), axis=0)
-            for t in range(TAPS))
-
-    terms = lax.fori_loop(0, K * R // SUB, kernel_body,
-                          tuple(jnp.zeros((8, C), jnp.float32) for _ in range(TAPS)))
-    kv[...] = jnp.zeros_like(kv)
-    for t in range(TAPS):
-        kv[t:t + 1, :] = jnp.sum(terms[t], axis=0, keepdims=True) * grad_scale
     for j in range(J):
-        kp[j] = jnp.concatenate([kv[:, j * cl:(j + 1) * cl], jnp.zeros((16, 128 - cl), jnp.float32)], axis=1)
+        ch = slice(j * cl, (j + 1) * cl)
+        sums = []
+        for t in range(TAPS):
+            acc = jnp.zeros((cl, R), jnp.float32)
+            for k in range(K):
+                acc = acc + (ge[ch, own + k * R:own + (k + 1) * R].astype(jnp.float32)
+                             * xe[ch, (k + t) * R:(k + t + 1) * R].astype(jnp.float32))
+            sums.append(jnp.sum(acc, axis=1, keepdims=True) * grad_scale)
+        kp[j] = jnp.concatenate(sums + [jnp.zeros((cl, 128 - TAPS), jnp.float32)], axis=1)
     k_in = to_chan(kp, kr)
 
     ge_left.wait_recv()
@@ -362,17 +354,14 @@
 
     def back_body(tile, carry):
         base = pl.multiple_of(tile * TILE, TILE)
-        for b in range(R // SUB):
-            pair = []
-            for h in range(2):
-                off = base + h * R + b * SUB
-                acc = ctf[pl.ds(off, SUB), :].astype(jnp.float32)
+        for h in range(TILE_STEPS):
+            off = base + h * R
+            for j in range(J):
+                ch = slice(j * cl, (j + 1) * cl)
+                acc = ctf[j, :, pl.ds(off, R)].astype(jnp.float32)
                 for t in range(TAPS):
-                    acc = acc + tf[t:t + 1, :] * ge[pl.ds(off + (TAPS - 1 - t) * R, SUB), :].astype(jnp.float32)
-                pair.append(acc.astype(jnp.bfloat16))
-            at = pl.ds(pl.multiple_of(tile * R, R) + b * SUB, SUB)
-            for j in range(J):
-                gs[j, at, :] = jnp.concatenate([p[:, j * cl:(j + 1) * cl] for p in pair], axis=1)
+                    acc = acc + tf[t, ch, :] * ge[ch, pl.ds(off + (TAPS - 1 - t) * R, R)].astype(jnp.float32)
+                gs[j, :, pl.ds(off, R)] = acc.astype(jnp.bfloat16)
         for c in tile_sends(gs, gr, gs_base, tile):
             c.start()
         return carry
@@ -414,10 +403,9 @@
                 c.wait_recv()
                 c.wait_send()
         for s in range(J):
-            for m in range(PAIRS):
-                for h in range(2):
-                    at = (2 * m + h) * DILATION_STEP + s * R
-                    out[at:at + R, :] = buf[s, m * R:(m + 1) * R, h * cl:(h + 1) * cl]
+            for k in range(K):
+                at = k * DILATION_STEP + s * R
+                out[:, at:at + R] = buf[s, :, k * R:(k + 1) * R]
 
     finish(bs, br, bo_base, bo_out)
     for c in h_in:
@@ -440,14 +428,14 @@
     total = kt[0]
     for l in range(1, L):
         total = total + kt[l]
-    gk_out[...] = total[0:TAPS, 0:cl]
+    gk_out[...] = total.T[0:TAPS, :]
     for c in z_in:
         c.wait_recv()
     total = sf[z]
     for e in range(1, Z):
         total = total + tr[lax.rem(z + Z - e, Z)]
     gw_in_out[...] = total[0]
-    gw_out_out[...] = total[1].T
+    gw_out_out[...] = total[1]
     for c in pending:
         c.wait_send()
 
@@ -455,7 +443,7 @@
 def fits(L, J, rows, cl, F):
     R = DILATION_STEP // J
     return (cl * 2 == 128 and rows == 2 * MIDDLE * DILATION_STEP and L % 2 == 0 and L > 2 and J > 1
-            and F == L * 128 and R % SUB == 0)
+            and F == L * 128 and R == 128)
 
 
 def fused_shards(features, kernel_tap_rows, in_weight, out_weight, cotangent):
@@ -471,20 +459,21 @@
     CR = C // J
     bf, f32 = jnp.bfloat16, jnp.float32
     ext = N + 2 * MIDDLE * R
-    packed = pltpu.VMEM((J, N // 2, 128), bf)
+    packed = pltpu.VMEM((J, cl, N), bf)
     scratch = [
         pltpu.VMEM((J, 16, 128), f32),
-        pltpu.VMEM((16, C), f32),
-        packed, packed,
-        pltpu.VMEM((ext, C), bf),
-        packed, packed,
-        pltpu.VMEM((N, C), bf),
-        pltpu.VMEM((N, C), bf),
-        pltpu.VMEM((2 * R, C), f32),
-        pltpu.VMEM((2 * R, 1), f32),
-        pltpu.VMEM((N, F), bf),
-        pltpu.VMEM((N, F), bf),
-        pltpu.VMEM((ext, C), bf),
+        pltpu.VMEM((TAPS, C, R), f32),
+        pltpu.VMEM((F, C), bf),
+        pltpu.VMEM((C, F), bf),
+        packed,
+        pltpu.VMEM((C, ext), bf),
+        packed, packed, packed,
+        pltpu.VMEM((C, N), bf),
+        pltpu.VMEM((C, 2 * R), f32),
+        pltpu.VMEM((1, 2 * R), f32),
+        pltpu.VMEM((F, N), bf),
+        pltpu.VMEM((F, N), bf),
+        pltpu.VMEM((C, ext), bf),
         packed, packed,
         packed, packed,
         pltpu.VMEM((2, Z, 2, C, 128), f32),
@@ -495,21 +484,20 @@
         pltpu.VMEM((J, Z, 2, CR, 128), bf),
         pltpu.VMEM((Z, 2, CR, 128), f32),
         pltpu.VMEM((Z, 2, CR, 128), f32),
-        pltpu.VMEM((16, C), f32),
-        pltpu.VMEM((J, 16, 128), f32),
-        pltpu.VMEM((J, 16, 128), f32),
-        pltpu.VMEM((L, 16, 128), f32),
+        pltpu.VMEM((J, cl, 128), f32),
+        pltpu.VMEM((J, cl, 128), f32),
+        pltpu.VMEM((L, cl, 128), f32),
     ]
     copies = (J - 1) * 5 + 4 + 2 * (K // 2) * (J - 1) + Z + (L - 1) + (Z - 1)
     scratch += [pltpu.SemaphoreType.DMA((copies,)), pltpu.SemaphoreType.DMA((copies,))]
     vmem = pl.BlockSpec(memory_space=pltpu.VMEM)
-    return pl.pallas_call(
+    bo, gx, gw_in, gw_out, gk = pl.pallas_call(
         functools.partial(fused_kernel, L, J, 1.0 / math.sqrt(rows * L)),
         out_shape=(
-            jax.ShapeDtypeStruct((rows, cl), bf),
-            jax.ShapeDtypeStruct((rows, cl), bf),
+            jax.ShapeDtypeStruct((cl, rows), bf),
+            jax.ShapeDtypeStruct((cl, rows), bf),
             jax.ShapeDtypeStruct((CR, F // L), f32),
-            jax.ShapeDtypeStruct((F // L, CR), f32),
+            jax.ShapeDtypeStruct((CR, F // L), f32),
             jax.ShapeDtypeStruct((TAPS, cl), f32),
         ),
         in_specs=[vmem] * 5,
@@ -518,7 +506,8 @@
         compiler_params=pltpu.CompilerParams(
             collective_id=0, has_side_effects=True, vmem_limit_bytes=50 * 1024 * 1024),
         cost_estimate=pl.CostEstimate(flops=12 * N * C * F, bytes_accessed=8 * rows * cl * 2, transcendentals=N * F),
-    )(features, cotangent, kernel_tap_rows, in_weight, out_weight)
+    )(features.T, cotangent.T, kernel_tap_rows, in_weight, out_weight)
+    return bo.T, gx.T, gw_in, gw_out.T, gk
 
 
 def solution(mesh):

time: 62.6 us -> 61.8 us (0.987)
  Pallas kernels: 53.8 us -> 52.5 us
    unnamed x12 -> x15, local copies, waits for them, and re-layouts: 4.99 us -> 8.27 us
    pallas_call x3 -> x0, local copies, waits for them, and re-layouts: 3.01 us -> none  [fused_shards(): pl.pallas_call(functools.partial(fused_kernel, L, J, 1.0 / math.sqrt(rows...]
    pallas_call x1, Pallas kernels: 53.8 us -> 52.5 us  [fused_shards(): pl.pallas_call(functools.partial(fused_kernel, L, J, 1.0 / math.sqrt(rows...]
where the time goes in v2:
time: 61.8 us; the launch traced here: 61.4 us
  Pallas kernels  52.5 us (85%)
  local copies, waits for them, and re-layouts  8.27 us (13%)
  between operations  0.66 us (1%)
    pallas_call x1, Pallas kernels, fused_shards(): pl.pallas_call(functools.partial(fused_kernel, L, J, 1.0 / math.sqrt(rows...  52.5 us
    unnamed x15, local copies, waits for them, and re-layouts  8.27 us

profile of v2, /device:TPU:0, one launch (start us, length us, event | category | flops | bytes accessed | tf_op | source)
XLA Modules:
  0.0 61.4 jit_solution(881725201988759851)
XLA Ops:
  0.6 0.0 copy-start
  0.6 1.0 %copy-done = bf16[4096,64]{0,1:T(8,128)(2,1)S(1)} copy-done((bf16[4096,64]{0,1:T(8,128)(2,1)S(1)}, bf16[4096,64]{0,1:T(8,128)(2,1)}, u32[]{:S(2)}) %copy-start) | copy-done | bytes 524312
  1.7 0.0 copy-start.1
  1.7 1.0 %copy-done.1 = bf16[4096,64]{0,1:T(8,128)(2,1)S(1)} copy-done((bf16[4096,64]{0,1:T(8,128)(2,1)S(1)}, bf16[4096,64]{0,1:T(8,128)(2,1)}, u32[]{:S(2)}) %copy-start.1) | copy-done | bytes 524312
  2.7 0.0 copy-start.2
  2.7 1.0 %copy-done.2 = bf16[256,1024]{1,0:T(8,128)(2,1)S(1)} copy-done((bf16[256,1024]{1,0:T(8,128)(2,1)S(1)}, bf16[256,1024]{1,0:T(8,128)(2,1)}, u32[]{:S(2)}) %copy-start.2) | copy-done | bytes 524312
  3.8 0.0 copy-start.3
  3.8 1.0 %copy-done.3 = bf16[1024,256]{1,0:T(8,128)(2,1)S(1)} copy-done((bf16[1024,256]{1,0:T(8,128)(2,1)S(1)}, bf16[1024,256]{1,0:T(8,128)(2,1)}, u32[]{:S(2)}) %copy-start.3) | copy-done | bytes 524312
  4.8 0.0 copy-start.4
  4.8 0.7 %copy-done.4 = f32[9,64]{1,0:T(8,128)S(1)} copy-done((f32[9,64]{1,0:T(8,128)S(1)}, f32[9,64]{1,0:T(8,128)}, u32[]{:S(2)}) %copy-start.4) | copy-done | bytes 2328
  5.5 52.5 %shard_map.92 = (bf16[64,4096]{1,0:T(8,128)(2,1)S(1)}, bf16[64,4096]{1,0:T(8,128)(2,1)S(1)}, f32[64,128]{1,0:T(8,128)S(1)}, f32[64,128]{1,0:T(8,128)S(1)}, f32[9,64]{1,0:T(8,128)S(1)}) custom-call(bf16[64,4096]{1,0:T(8,128)(2,1)S(1)} %bitcast.8, bf16[64,4096]{1,0:T(8,128)(2,1)S(1)} %bitcast.9, f32[9,64]{1,0:T(8,128)S(1)} %copy-done.4, ...), custom_call_target="tpu_custom_call" | custom-call | flops 3221225472 | bytes 4194304 | tf_op jit(solution)/shard_map/pallas_call | solution.py:494
  58.0 0.8 %copy.15 = bf16[4096,64]{0,1:T(8,128)(2,1)} copy(bf16[4096,64]{0,1:T(8,128)(2,1)S(1)} %bitcast.6) | data formatting | bytes 1048576
  58.8 0.8 %copy.16 = bf16[4096,64]{0,1:T(8,128)(2,1)} copy(bf16[4096,64]{0,1:T(8,128)(2,1)S(1)} %bitcast.5) | data formatting | bytes 1048576
  59.6 0.6 copy.17
  60.2 0.6 copy.18
  60.8 0.6 copy.19
Async XLA Ops:
  0.6 1.0 %copy-start = (bf16[4096,64]{0,1:T(8,128)(2,1)S(1)}, bf16[4096,64]{0,1:T(8,128)(2,1)}, u32[]{:S(2)}) copy-start(bf16[4096,64]{0,1:T(8,128)(2,1)} %param.5) | copy-start | bytes 1572868
  1.7 1.0 %copy-start.1 = (bf16[4096,64]{0,1:T(8,128)(2,1)S(1)}, bf16[4096,64]{0,1:T(8,128)(2,1)}, u32[]{:S(2)}) copy-start(bf16[4096,64]{0,1:T(8,128)(2,1)} %param.9) | copy-start | bytes 1572868
  2.7 1.0 %copy-start.2 = (bf16[256,1024]{1,0:T(8,128)(2,1)S(1)}, bf16[256,1024]{1,0:T(8,128)(2,1)}, u32[]{:S(2)}) copy-start(bf16[256,1024]{1,0:T(8,128)(2,1)} %win.1) | copy-start | bytes 1572868
  3.8 1.0 %copy-start.3 = (bf16[1024,256]{1,0:T(8,128)(2,1)S(1)}, bf16[1024,256]{1,0:T(8,128)(2,1)}, u32[]{:S(2)}) copy-start(bf16[1024,256]{1,0:T(8,128)(2,1)} %wout.1) | copy-start | bytes 1572868
  4.8 0.7 %copy-start.4 = (f32[9,64]{1,0:T(8,128)S(1)}, f32[9,64]{1,0:T(8,128)}, u32[]{:S(2)}) copy-start(f32[9,64]{1,0:T(8,128)} %taps.1) | copy-start | bytes 6916

commit v3 on v2

--- a/solution.py
+++ b/solution.py
@@ -159,12 +159,16 @@
 
 def fused_kernel(
     L, J, grad_scale,
-    x, ct, taps, win, wout,
+    x_hbm, ct_hbm, taps_hbm, win_hbm, wout_hbm,
     bo_out, gx_out, gw_in_out, gw_out_out, gk_out,
     tb, tf, wint, woutt, xs, xe, cs, ctf, xr, nb, nrm, istd, act, gp, ge,
     bs, br, gs, gr, gfull, gsend, grecv, hf, hs, hr, sf, tr, kp, kr, kt,
-    send, recv,
+    x, ct, taps, win, wout, load, send, recv,
 ):
+    loads = [pltpu.make_async_copy(a, b, load.at[i]) for i, (a, b) in enumerate(
+        ((x_hbm, x), (taps_hbm, taps), (ct_hbm, ct), (win_hbm, win), (wout_hbm, wout)))]
+    for c in loads:
+        c.start()
     cl, rows = x.shape
     C = cl * J
     F = win.shape[1]
@@ -203,6 +207,8 @@
                 a = k * DILATION_STEP + j * R
                 dst[j, :, k * R:(k + 1) * R] = src[:, a:a + R]
 
+    loads[0].wait()
+    loads[1].wait()
     tb[me_j] = jnp.zeros((16, 128), jnp.float32)
     tb[me_j, 0:TAPS, 0:cl] = taps[...]
     pack(x, xs)
@@ -226,9 +232,12 @@
         c.start()
         tap_in.append(c)
     pending.extend(tap_in)
+    loads[2].wait()
     pack(ct, cs)
     ct_in = to_chan(cs, ctf)
 
+    loads[3].wait()
+    loads[4].wait()
     wint[...] = win[...].T
     woutt[...] = wout[...].T
     xr[me_j] = xs[me_j]
@@ -489,6 +498,14 @@
         pltpu.VMEM((L, cl, 128), f32),
     ]
     copies = (J - 1) * 5 + 4 + 2 * (K // 2) * (J - 1) + Z + (L - 1) + (Z - 1)
+    scratch += [
+        pltpu.VMEM((cl, rows), bf),
+        pltpu.VMEM((cl, rows), bf),
+        pltpu.VMEM((TAPS, cl), f32),
+        pltpu.VMEM((C, F), bf),
+        pltpu.VMEM((F, C), bf),
+        pltpu.SemaphoreType.DMA((5,)),
+    ]
     scratch += [pltpu.SemaphoreType.DMA((copies,)), pltpu.SemaphoreType.DMA((copies,))]
     vmem = pl.BlockSpec(memory_space=pltpu.VMEM)
     bo, gx, gw_in, gw_out, gk = pl.pallas_call(
@@ -500,7 +517,7 @@
             jax.ShapeDtypeStruct((CR, F // L), f32),
             jax.ShapeDtypeStruct((TAPS, cl), f32),
         ),
-        in_specs=[vmem] * 5,
+        in_specs=[pl.BlockSpec(memory_space=pltpu.HBM)] * 5,
         out_specs=(vmem,) * 5,
         scratch_shapes=scratch,
         compiler_params=pltpu.CompilerParams(

time: 61.8 us -> 62 us (level)
  no operation moved by 1% of the time
where the time goes in v3:
time: 62 us; the launch traced here: 61.6 us
  Pallas kernels  52.7 us (85%)
  local copies, waits for them, and re-layouts  8.27 us (13%)
  between operations  0.66 us (1%)
    pallas_call x1, Pallas kernels, fused_shards(): pl.pallas_call(functools.partial(fused_kernel, L, J, 1.0 / math.sqrt(rows...  52.7 us
    unnamed x15, local copies, waits for them, and re-layouts  8.27 us

profile of v3, /device:TPU:0, one launch (start us, length us, event | category | flops | bytes accessed | tf_op | source)
XLA Modules:
  0.0 61.6 jit_solution(10254860930739277194)
XLA Ops:
  0.6 0.0 copy-start
  0.6 1.0 %copy-done = bf16[4096,64]{0,1:T(8,128)(2,1)S(1)} copy-done((bf16[4096,64]{0,1:T(8,128)(2,1)S(1)}, bf16[4096,64]{0,1:T(8,128)(2,1)}, u32[]{:S(2)}) %copy-start) | copy-done | bytes 524312
  1.7 0.0 copy-start.1
  1.7 1.0 %copy-done.1 = bf16[4096,64]{0,1:T(8,128)(2,1)S(1)} copy-done((bf16[4096,64]{0,1:T(8,128)(2,1)S(1)}, bf16[4096,64]{0,1:T(8,128)(2,1)}, u32[]{:S(2)}) %copy-start.1) | copy-done | bytes 524312
  2.7 0.0 copy-start.2
  2.7 1.0 %copy-done.2 = bf16[256,1024]{1,0:T(8,128)(2,1)S(1)} copy-done((bf16[256,1024]{1,0:T(8,128)(2,1)S(1)}, bf16[256,1024]{1,0:T(8,128)(2,1)}, u32[]{:S(2)}) %copy-start.2) | copy-done | bytes 524312
  3.8 0.0 copy-start.3
  3.8 1.0 %copy-done.3 = bf16[1024,256]{1,0:T(8,128)(2,1)S(1)} copy-done((bf16[1024,256]{1,0:T(8,128)(2,1)S(1)}, bf16[1024,256]{1,0:T(8,128)(2,1)}, u32[]{:S(2)}) %copy-start.3) | copy-done | bytes 524312
  4.8 0.0 copy-start.4
  4.8 0.7 %copy-done.4 = f32[9,64]{1,0:T(8,128)S(1)} copy-done((f32[9,64]{1,0:T(8,128)S(1)}, f32[9,64]{1,0:T(8,128)}, u32[]{:S(2)}) %copy-start.4) | copy-done | bytes 2328
  5.5 52.7 %shard_map.92 = (bf16[64,4096]{1,0:T(8,128)(2,1)S(1)}, bf16[64,4096]{1,0:T(8,128)(2,1)S(1)}, f32[64,128]{1,0:T(8,128)S(1)}, f32[64,128]{1,0:T(8,128)S(1)}, f32[9,64]{1,0:T(8,128)S(1)}) custom-call(bf16[64,4096]{1,0:T(8,128)(2,1)S(1)} %bitcast.8, bf16[64,4096]{1,0:T(8,128)(2,1)S(1)} %bitcast.9, f32[9,64]{1,0:T(8,128)S(1)} %copy-done.4, ...), custom_call_target="tpu_custom_call" | custom-call | flops 3221225472 | bytes 4194304 | tf_op jit(solution)/shard_map/pallas_call | solution.py:511
  58.2 0.8 %copy.15 = bf16[4096,64]{0,1:T(8,128)(2,1)} copy(bf16[4096,64]{0,1:T(8,128)(2,1)S(1)} %bitcast.6) | data formatting | bytes 1048576
  59.0 0.8 %copy.16 = bf16[4096,64]{0,1:T(8,128)(2,1)} copy(bf16[4096,64]{0,1:T(8,128)(2,1)S(1)} %bitcast.5) | data formatting | bytes 1048576
  59.8 0.6 copy.17
  60.4 0.6 copy.18
  61.0 0.6 copy.19
Async XLA Ops:
  0.6 1.0 %copy-start = (bf16[4096,64]{0,1:T(8,128)(2,1)S(1)}, bf16[4096,64]{0,1:T(8,128)(2,1)}, u32[]{:S(2)}) copy-start(bf16[4096,64]{0,1:T(8,128)(2,1)} %param.5) | copy-start | bytes 1572868
  1.7 1.0 %copy-start.1 = (bf16[4096,64]{0,1:T(8,128)(2,1)S(1)}, bf16[4096,64]{0,1:T(8,128)(2,1)}, u32[]{:S(2)}) copy-start(bf16[4096,64]{0,1:T(8,128)(2,1)} %param.9) | copy-start | bytes 1572868
  2.7 1.0 %copy-start.2 = (bf16[256,1024]{1,0:T(8,128)(2,1)S(1)}, bf16[256,1024]{1,0:T(8,128)(2,1)}, u32[]{:S(2)}) copy-start(bf16[256,1024]{1,0:T(8,128)(2,1)} %win_hbm.1) | copy-start | bytes 1572868
  3.8 1.0 %copy-start.3 = (bf16[1024,256]{1,0:T(8,128)(2,1)S(1)}, bf16[1024,256]{1,0:T(8,128)(2,1)}, u32[]{:S(2)}) copy-start(bf16[1024,256]{1,0:T(8,128)(2,1)} %wout_hbm.1) | copy-start | bytes 1572868
  4.8 0.7 %copy-start.4 = (f32[9,64]{1,0:T(8,128)S(1)}, f32[9,64]{1,0:T(8,128)}, u32[]{:S(2)}) copy-start(f32[9,64]{1,0:T(8,128)} %taps_hbm.1) | copy-start | bytes 6916

commit v4 on v2

--- a/solution.py
+++ b/solution.py
@@ -336,18 +336,6 @@
 
     lax.fori_loop(0, Z, term_body, 0)
 
-    for j in range(J):
-        ch = slice(j * cl, (j + 1) * cl)
-        sums = []
-        for t in range(TAPS):
-            acc = jnp.zeros((cl, R), jnp.float32)
-            for k in range(K):
-                acc = acc + (ge[ch, own + k * R:own + (k + 1) * R].astype(jnp.float32)
-                             * xe[ch, (k + t) * R:(k + t + 1) * R].astype(jnp.float32))
-            sums.append(jnp.sum(acc, axis=1, keepdims=True) * grad_scale)
-        kp[j] = jnp.concatenate(sums + [jnp.zeros((cl, 128 - TAPS), jnp.float32)], axis=1)
-    k_in = to_chan(kp, kr)
-
     ge_left.wait_recv()
     ge_right.wait_recv()
     pending.extend([ge_left, ge_right])
@@ -367,6 +355,18 @@
         return carry
 
     lax.fori_loop(0, PAIRS, back_body, 0)
+
+    for j in range(J):
+        ch = slice(j * cl, (j + 1) * cl)
+        sums = []
+        for t in range(TAPS):
+            acc = jnp.zeros((cl, R), jnp.float32)
+            for k in range(K):
+                acc = acc + (ge[ch, own + k * R:own + (k + 1) * R].astype(jnp.float32)
+                             * xe[ch, (k + t) * R:(k + t + 1) * R].astype(jnp.float32))
+            sums.append(jnp.sum(acc, axis=1, keepdims=True) * grad_scale)
+        kp[j] = jnp.concatenate(sums + [jnp.zeros((cl, 128 - TAPS), jnp.float32)], axis=1)
+    k_in = to_chan(kp, kr)
 
     CR = C // J
 

time: 61.8 us -> 63.8 us (1.032)
  Pallas kernels: 52.5 us -> 54.5 us
    pallas_call x1, Pallas kernels: 52.5 us -> 54.5 us  [fused_shards(): pl.pallas_call(functools.partial(fused_kernel, L, J, 1.0 / math.sqrt(rows...]
where the time goes in v4:
time: 63.8 us; the launch traced here: 63.4 us
  Pallas kernels  54.5 us (85%)
  local copies, waits for them, and re-layouts  8.27 us (13%)
  between operations  0.66 us (1%)
    pallas_call x1, Pallas kernels, fused_shards(): pl.pallas_call(functools.partial(fused_kernel, L, J, 1.0 / math.sqrt(rows...  54.5 us
    unnamed x15, local copies, waits for them, and re-layouts  8.27 us

profile of v4, /device:TPU:0, one launch (start us, length us, event | category | flops | bytes accessed | tf_op | source)
XLA Modules:
  0.0 63.4 jit_solution(5484034184085013218)
XLA Ops:
  0.6 0.0 copy-start
  0.6 1.0 %copy-done = bf16[4096,64]{0,1:T(8,128)(2,1)S(1)} copy-done((bf16[4096,64]{0,1:T(8,128)(2,1)S(1)}, bf16[4096,64]{0,1:T(8,128)(2,1)}, u32[]{:S(2)}) %copy-start) | copy-done | bytes 524312
  1.7 0.0 copy-start.1
  1.7 1.0 %copy-done.1 = bf16[4096,64]{0,1:T(8,128)(2,1)S(1)} copy-done((bf16[4096,64]{0,1:T(8,128)(2,1)S(1)}, bf16[4096,64]{0,1:T(8,128)(2,1)}, u32[]{:S(2)}) %copy-start.1) | copy-done | bytes 524312
  2.7 0.0 copy-start.2
  2.7 1.0 %copy-done.2 = bf16[256,1024]{1,0:T(8,128)(2,1)S(1)} copy-done((bf16[256,1024]{1,0:T(8,128)(2,1)S(1)}, bf16[256,1024]{1,0:T(8,128)(2,1)}, u32[]{:S(2)}) %copy-start.2) | copy-done | bytes 524312
  3.8 0.0 copy-start.3
  3.8 1.0 %copy-done.3 = bf16[1024,256]{1,0:T(8,128)(2,1)S(1)} copy-done((bf16[1024,256]{1,0:T(8,128)(2,1)S(1)}, bf16[1024,256]{1,0:T(8,128)(2,1)}, u32[]{:S(2)}) %copy-start.3) | copy-done | bytes 524312
  4.8 0.0 copy-start.4
  4.8 0.7 %copy-done.4 = f32[9,64]{1,0:T(8,128)S(1)} copy-done((f32[9,64]{1,0:T(8,128)S(1)}, f32[9,64]{1,0:T(8,128)}, u32[]{:S(2)}) %copy-start.4) | copy-done | bytes 2328
  5.5 54.5 %shard_map.92 = (bf16[64,4096]{1,0:T(8,128)(2,1)S(1)}, bf16[64,4096]{1,0:T(8,128)(2,1)S(1)}, f32[64,128]{1,0:T(8,128)S(1)}, f32[64,128]{1,0:T(8,128)S(1)}, f32[9,64]{1,0:T(8,128)S(1)}) custom-call(bf16[64,4096]{1,0:T(8,128)(2,1)S(1)} %bitcast.8, bf16[64,4096]{1,0:T(8,128)(2,1)S(1)} %bitcast.9, f32[9,64]{1,0:T(8,128)S(1)} %copy-done.4, ...), custom_call_target="tpu_custom_call" | custom-call | flops 3221225472 | bytes 4194304 | tf_op jit(solution)/shard_map/pallas_call | solution.py:494
  60.0 0.8 %copy.15 = bf16[4096,64]{0,1:T(8,128)(2,1)} copy(bf16[4096,64]{0,1:T(8,128)(2,1)S(1)} %bitcast.6) | data formatting | bytes 1048576
  60.8 0.8 %copy.16 = bf16[4096,64]{0,1:T(8,128)(2,1)} copy(bf16[4096,64]{0,1:T(8,128)(2,1)S(1)} %bitcast.5) | data formatting | bytes 1048576
  61.6 0.6 copy.17
  62.2 0.6 copy.18
  62.8 0.6 copy.19
Async XLA Ops:
  0.6 1.0 %copy-start = (bf16[4096,64]{0,1:T(8,128)(2,1)S(1)}, bf16[4096,64]{0,1:T(8,128)(2,1)}, u32[]{:S(2)}) copy-start(bf16[4096,64]{0,1:T(8,128)(2,1)} %param.5) | copy-start | bytes 1572868
  1.7 1.0 %copy-start.1 = (bf16[4096,64]{0,1:T(8,128)(2,1)S(1)}, bf16[4096,64]{0,1:T(8,128)(2,1)}, u32[]{:S(2)}) copy-start(bf16[4096,64]{0,1:T(8,128)(2,1)} %param.9) | copy-start | bytes 1572868
  2.7 1.0 %copy-start.2 = (bf16[256,1024]{1,0:T(8,128)(2,1)S(1)}, bf16[256,1024]{1,0:T(8,128)(2,1)}, u32[]{:S(2)}) copy-start(bf16[256,1024]{1,0:T(8,128)(2,1)} %win.1) | copy-start | bytes 1572868
  3.8 1.0 %copy-start.3 = (bf16[1024,256]{1,0:T(8,128)(2,1)S(1)}, bf16[1024,256]{1,0:T(8,128)(2,1)}, u32[]{:S(2)}) copy-start(bf16[1024,256]{1,0:T(8,128)(2,1)} %wout.1) | copy-start | bytes 1572868
  4.8 0.7 %copy-start.4 = (f32[9,64]{1,0:T(8,128)S(1)}, f32[9,64]{1,0:T(8,128)}, u32[]{:S(2)}) copy-start(f32[9,64]{1,0:T(8,128)} %taps.1) | copy-start | bytes 6916
